TPU v7x, 32 devices: a whole 2x2x4 slice. The times are simulated.
32 devices in a mesh: parts: 2 (over y), blk: 4 (over z), lay: 4 (over x, core).
Axes of the slice: x: 2, y: 2, z: 4, core: 2. Of those that a mesh axis runs over, the one named last changes fastest.
Arguments:
- query_grads: bfloat16 [1024, 4, 4096], P(('parts', 'blk'), 'lay'), parts along dimension 0, may hold values from -6 to 6
- train_grads: bfloat16 [2048, 4, 4096], P(('parts', 'blk'), 'lay'), parts along dimension 0, may hold values from -6 to 6
- basis_out: float32 [4, 64, 64], P('lay'), may hold values from -0.75 to 0.75
- basis_in: float32 [4, 64, 64], P('lay'), may hold values from -0.75 to 0.75
- spectrum: float32 [4, 4096], P('lay'), may hold values from 0.3 to 10
- train_ids: int32 [8, 256], P(('parts', 'blk')), parts along dimension 0, may hold values from 0 to 255, each once within a row
Outputs:
- scores: float32 [1024, 1024], P(('parts', 'lay'), 'blk'), parts along dimension 0
There are 2 independent parts, one for each index of `parts`. A program takes and returns all parts, laid end to end along the dimension named above; an argument that names none is the same for every part. Nothing has to cross between parts.
Inputs may be any that keep to these rules, and one draw needn't show every extreme that they name: Each row of train_ids holds every number of 0 to 255 once.
All inputs are finite; a program needn't handle non-finite values.
Results may differ from a plain program's by a relative error of at most 0.0029.
Values may be sent and summed in bfloat16 or wider, within the bound.
A program may use at most 128 MiB of HBM per device.

v0:
```python
import jax
import jax.numpy as jnp
from jax import lax
from jax.sharding import PartitionSpec as P

damping = 0.1
score_scale = 1.0 / 256.0


def precondition(grads, basis_out, basis_in, spectrum):
    row_count = grads.shape[0]
    lay_count = grads.shape[1]
    out_dim = basis_out.shape[1]
    in_dim = basis_in.shape[1]
    field = grads.astype(jnp.float32).reshape(row_count, lay_count, out_dim, in_dim)
    high = lax.Precision.HIGHEST
    rotated = jnp.einsum("lap,mlab->mlpb", basis_out, field, precision=high)
    rotated = jnp.einsum("mlpb,lbr->mlpr", rotated, basis_in, precision=high)
    scaled = rotated / (spectrum.reshape(1, lay_count, out_dim, in_dim) + damping)
    restored = jnp.einsum("lap,mlpr->mlar", basis_out, scaled, precision=high)
    restored = jnp.einsum("mlar,lbr->mlab", restored, basis_in, precision=high)
    return restored.reshape(row_count, lay_count * out_dim * in_dim).astype(jnp.bfloat16)


def per_device(query_grads, train_grads, basis_out, basis_in, spectrum, train_ids):
    prepared = precondition(query_grads, basis_out, basis_in, spectrum)
    local_rows = train_grads.reshape(train_grads.shape[0], -1)
    all_queries = lax.all_gather(prepared, "blk", axis=0, tiled=True)
    summed = lax.psum_scatter(
        lax.dot_general(
            all_queries, local_rows, (((1,), (1,)), ((), ())), preferred_element_type=jnp.float32
        ),
        "lay",
        scatter_dimension=0,
        tiled=True,
    )
    scaled_scores = summed * score_scale
    return jnp.take(scaled_scores, train_ids[0], axis=1)


def solution(mesh):
    in_specs = (
        P(("parts", "blk"), "lay", None),
        P(("parts", "blk"), "lay", None),
        P("lay", None, None),
        P("lay", None, None),
        P("lay", None),
        P(("parts", "blk"), None),
    )
    out_specs = P(("parts", "lay"), "blk")
    return jax.shard_map(
        per_device, mesh=mesh, in_specs=in_specs, out_specs=out_specs, check_vma=False
    )
```

profile of v0, /device:TPU:0, one launch (start us, length us, event | category | flops | bytes accessed | tf_op | source)
XLA Modules:
  0.0 138.9 jit_solution(1306738713858230764)
XLA Ops:
  6.5 0.0 copy-start
  6.5 0.0 copy-start.3
  6.5 0.0 copy-start.1
  6.5 0.0 all-gather.2.cloned.1.call-start
  6.5 1.8 %copy.15 = bf16[128,1,4096]{0,2,1:T(8,128)(2,1)S(1)} copy(bf16[128,1,4096]{2,0,1:T(8,128)(2,1)} %param.6) | data formatting | bytes 2097152 | tf_op args[0]
  8.3 0.0 copy-done.3
  8.3 0.0 copy-start.2
  8.4 0.1 add.41
  8.5 0.0 copy-done.1
  8.5 1.4 %convolution_bitcast_fusion = f32[128,64,64]{0,1,2:T(8,128)S(1)} fusion(bf16[128,64,64]{0,2,1:T(8,128)(2,1)S(1)} %bitcast.57, f32[1,64,64]{2,1,0:T(8,128)S(1)} %copy-done.1), kind=kOutput, calls=%fused_computation.12 | convolution fusion | flops 402653184 | bytes 3162112 | tf_op jit(solution)/shard_map/lap,mlab->mlpb/dot_general | solution.py:17
  9.9 0.0 copy-done.2
  9.9 4.2 %fusion = f32[128,64,64]{0,2,1:T(8,128)S(1)} fusion(f32[128,64,64]{0,1,2:T(8,128)S(1)} %convolution_bitcast_fusion, f32[64,64]{1,0:T(8,128)S(1)} %add.41, f32[1,64,64]{2,1,0:T(8,128)S(1)} %copy-done.2), kind=kOutput, calls=%fused_computation.2 | convolution fusion | flops 403177472 | bytes 4227072 | tf_op jit(solution)/shard_map/mlpb,lbr->mlpr/dot_general | solution.py:18
  14.1 3.3 %fusion.9 = f32[128,64,64]{0,1,2:T(8,128)S(1)} fusion(f32[128,64,64]{0,2,1:T(8,128)S(1)} %fusion, f32[1,64,64]{2,1,0:T(8,128)S(1)} %copy-done.1), kind=kOutput, calls=%fused_computation.11 | convolution fusion | flops 402653184 | bytes 4210688 | tf_op jit(solution)/shard_map/lap,mlpr->mlar/dot_general | solution.py:20
  17.4 4.3 %fusion.14 = bf16[128,64,64]{0,2,1:T(8,128)(2,1)} fusion(f32[128,64,64]{0,1,2:T(8,128)S(1)} %fusion.9, f32[1,64,64]{2,1,0:T(8,128)S(1)} %copy-done.2), kind=kOutput, calls=%fused_computation.13 | convolution fusion | flops 403177472 | bytes 3162112 | tf_op jit(solution)/shard_map/mlar,lbr->mlab/dot_general | solution.py:21
  21.7 0.0 all-gather.2.cloned.1.call-update
  21.7 0.0 copy-start.4
  21.7 0.0 reduce-scatter.2.cloned.1.call-start
  21.7 83.4 %all-gather.2.cloned.1.call-done = bf16[512,4096]{0,1:T(8,128)(2,1)} async-done(((bf16[128,4096]{0,1:T(8,128)(2,1)}), bf16[512,4096]{0,1:T(8,128)(2,1)}) %all-gather.2.cloned.1.call-update) | async-done | bytes 4194320 | tf_op jit(solution)/shard_map/all_gather | solution.py:28
  105.1 0.0 copy-done
  105.1 4.3 %fusion.1 = f32[512,256]{1,0:T(8,128)} fusion(bf16[512,4096]{0,1:T(8,128)(2,1)} %all-gather.2.cloned.1.call-done, bf16[256,1,4096]{2,0,1:T(8,128)(2,1)S(1)} %copy-done), kind=kOutput, calls=%fused_computation.3 | convolution fusion | flops 1073741824 | bytes 6815744 | tf_op jit(solution)/shard_map/dot_general | solution.py:30
  109.4 0.0 reduce-scatter.2.cloned.1.call-update
  109.4 0.0 copy-done.4
  109.5 20.0 %reduce-scatter.2.cloned.1.call-done = f32[128,256]{1,0:T(8,128)} async-done(((f32[512,256]{1,0:T(8,128)}), f32[128,256]{1,0:T(8,128)}) %reduce-scatter.2.cloned.1.call-update) | async-done | bytes 131088 | tf_op jit(solution)/shard_map/reduce_scatter | solution.py:29
  129.4 0.9 broadcast_multiply_fusion
  130.4 0.1 copy.22
  130.5 0.7 gather_fusion
  131.2 0.1 select_bitcast_fusion
  131.3 0.8 copy.23
  (4 shorter events, 0.1 us)
Async XLA Ops:
  6.5 98.6 %copy-start = (bf16[256,1,4096]{2,0,1:T(8,128)(2,1)S(1)}, bf16[256,1,4096]{2,0,1:T(8,128)(2,1)}, u32[]{:S(2)}) copy-start(bf16[256,1,4096]{2,0,1:T(8,128)(2,1)} %param.7) | copy-start | bytes 6291460
  6.5 1.8 %copy-start.3 = (f32[1,4096]{1,0:T(1,128)S(1)}, f32[1,4096]{1,0:T(1,128)}, u32[]{:S(2)}) copy-start(f32[1,4096]{1,0:T(1,128)} %param.10) | copy-start | bytes 49156
  6.5 1.9 %copy-start.1 = (f32[1,64,64]{2,1,0:T(8,128)S(1)}, f32[1,64,64]{2,1,0:T(8,128)}, u32[]{:S(2)}) copy-start(f32[1,64,64]{2,1,0:T(8,128)} %param.8) | copy-start | bytes 49156
  6.5 98.6 %all-gather.2.cloned.1.call-start = ((), (), s32[]{:S(2)}) async-start(), calls=%async_computation.1 | async-start | bytes 5242880 | tf_op jit(solution)/shard_map/all_gather | solution.py:28
  8.3 1.6 %copy-start.2 = (f32[1,64,64]{2,1,0:T(8,128)S(1)}, f32[1,64,64]{2,1,0:T(8,128)}, u32[]{:S(2)}) copy-start(f32[1,64,64]{2,1,0:T(8,128)} %param.9) | copy-start | bytes 49156
  21.7 87.8 %copy-start.4 = (s32[1,256]{1,0:T(1,128)S(1)}, s32[1,256]{1,0:T(1,128)}, u32[]{:S(2)}) copy-start(s32[1,256]{1,0:T(1,128)} %param.11) | copy-start | bytes 3076
  21.7 107.8 %reduce-scatter.2.cloned.1.call-start = ((), (), s32[]{:S(2)}) async-start(), calls=%async_computation.2 | async-start | bytes 655360 | tf_op jit(solution)/shard_map/reduce_scatter | solution.py:29
Sparse Core Ops, SparseCore 0:
  21.8 83.2 all-gather.1
  109.6 19.8 reduce-scatter.1
where the time goes:
time: 139 us
  waiting for transfers between devices  103 us (74%)
  matrix products  17.4 us (13%)
  between operations  13.5 us (10%)
  local copies, waits for them, and re-layouts  3.44 us (2%)
    all_gather x1, waiting for transfers between devices, per_device(): all_queries = lax.all_gather(prepared, 'blk', axis=0, tiled=True)  83.4 us
    reduce_scatter x1, waiting for transfers between devices, per_device(): lax.psum_scatter(lax.dot_general(all_queries, local_rows, (((1,), (1,)),...  20 us
    dot_general x1, matrix products, per_device(): lax.dot_general(all_queries, local_rows, (((1,), (1,)), ((), ())), prefer...  4.3 us
    dot_general x1, matrix products, precondition(): restored = jnp.einsum('mlar,lbr->mlab', restored, basis_in, precision=high)  4.25 us
    dot_general x1, matrix products, precondition(): rotated = jnp.einsum('mlpb,lbr->mlpr', rotated, basis_in, precision=high)  4.18 us
    dot_general x1, matrix products, precondition(): restored = jnp.einsum('lap,mlpr->mlar', basis_out, scaled, precision=high)  3.28 us
  transfers between devices with their start and end apart: 2, of which 2 were waited for; matrix products, arithmetic and copies ran while one was open for 0% of the time, Pallas kernels for 0%

commit v1 on v0

--- a/solution.py
+++ b/solution.py
@@ -1,10 +1,17 @@
+import functools
+
 import jax
 import jax.numpy as jnp
 from jax import lax
+from jax.experimental import pallas as pl
+from jax.experimental.pallas import tpu as pltpu
 from jax.sharding import PartitionSpec as P
 
 damping = 0.1
 score_scale = 1.0 / 256.0
+MESH = pl.DeviceIdType.MESH
+f32 = jnp.float32
+bf16 = jnp.bfloat16
 
 
 def precondition(grads, basis_out, basis_in, spectrum):
@@ -22,7 +29,7 @@
     return restored.reshape(row_count, lay_count * out_dim * in_dim).astype(jnp.bfloat16)
 
 
-def per_device(query_grads, train_grads, basis_out, basis_in, spectrum, train_ids):
+def plain(query_grads, train_grads, basis_out, basis_in, spectrum, train_ids):
     prepared = precondition(query_grads, basis_out, basis_in, spectrum)
     local_rows = train_grads.reshape(train_grads.shape[0], -1)
     all_queries = lax.all_gather(prepared, "blk", axis=0, tiled=True)
@@ -38,6 +45,273 @@
     return jnp.take(scaled_scores, train_ids[0], axis=1)
 
 
+def dot(a, b, dims=((1,), (0,))):
+    return lax.dot_general(a, b, (dims, ((), ())), preferred_element_type=f32)
+
+
+def split(x):
+    hi = x.astype(bf16)
+    return hi, (x - hi.astype(f32)).astype(bf16)
+
+
+def dot3(a_hi, a_lo, b):
+    b_hi, b_lo = split(b)
+    return dot(a_hi, b_hi) + (dot(a_hi, b_lo) + dot(a_lo, b_hi))
+
+
+CH = 16
+GR = 64
+SIDE = 64
+TILE = 256
+
+
+def kernel(n, q_hbm, t_hbm, bo_ref, bi_ref, sp_ref, ids_ref, o_ref,
+           q_all, t_ref, x_ref, tp_hi, tp_lo, perm, diag, stage, red,
+           load_sem, send_sem, recv_sem, rsend_sem, rrecv_sem):
+    z = lax.axis_index("blk")
+    l = lax.axis_index("lay")
+    rows = q_hbm.shape[0]
+    cols = t_ref.shape[0]
+    width = q_hbm.shape[1]
+    tiles = width // TILE
+    C = rows // CH
+    G = rows // GR
+    T = (n - 1) * C
+
+    own = pltpu.make_async_copy(
+        q_hbm, q_all.at[pl.ds(pl.multiple_of(z * rows, rows), rows), :], load_sem.at[0])
+    own.start()
+    train = pltpu.make_async_copy(t_hbm, t_ref, load_sem.at[1])
+    train.start()
+
+    barrier = pltpu.get_barrier_semaphore()
+
+    @pl.when(z > 0)
+    def _():
+        pl.semaphore_signal(barrier, inc=1, device_id={"blk": z - 1}, device_id_type=MESH)
+
+    @pl.when(z < n - 1)
+    def _():
+        pl.semaphore_signal(barrier, inc=1, device_id={"blk": z + 1}, device_id_type=MESH)
+
+    for k in range(1, n):
+        pl.semaphore_signal(
+            barrier, inc=1, device_id={"lay": lax.rem(l + k, n)}, device_id_type=MESH)
+
+    row_i = lax.broadcasted_iota(jnp.int32, (TILE, SIDE), 0)
+    col_i = lax.broadcasted_iota(jnp.int32, (TILE, SIDE), 1)
+    pick = jnp.where(lax.rem(row_i, SIDE) == col_i, 1.0, 0.0).astype(bf16)
+    big_r = lax.broadcasted_iota(jnp.int32, (TILE, TILE), 0)
+    big_c = lax.broadcasted_iota(jnp.int32, (TILE, TILE), 1)
+    same = big_r // SIDE == big_c // SIDE
+
+    def spread(base, side):
+        half = dot(pick, base, ((1,), (side,))).astype(bf16)
+        full = dot(half, pick, ((1,), (1,)))
+        return jnp.where(same, full, 0.0).astype(bf16)
+
+    for k, (ref, side) in enumerate(((bi_ref, 1), (bo_ref, 1), (bo_ref, 0), (bi_ref, 0))):
+        hi, lo = split(ref[...])
+        diag[2 * k] = spread(hi, side)
+        diag[2 * k + 1] = spread(lo, side)
+    perm[...] = jnp.where(big_r == ids_ref[...], 1.0, 0.0).astype(bf16)
+
+    own.wait()
+    train.wait()
+    pl.semaphore_wait(
+        barrier, (n - 1) + (z > 0).astype(jnp.int32) + (z < n - 1).astype(jnp.int32))
+
+    def chunk(block, c):
+        return q_all.at[pl.ds(pl.multiple_of(block * rows + c * CH, CH), CH), :]
+
+    def copy(way, t, block, target):
+        part = chunk(block, lax.rem(t, C))
+        return pltpu.make_async_remote_copy(
+            src_ref=part, dst_ref=part, send_sem=send_sem.at[way, t],
+            recv_sem=recv_sem.at[way, t], device_id={"blk": target}, device_id_type=MESH)
+
+    def send_right(t):
+        return copy(0, t, z - t // C, z + 1)
+
+    def send_left(t):
+        return copy(1, t, z + t // C, z - 1)
+
+    def from_left(t):
+        return copy(0, t, z - 1 - t // C, z + 1)
+
+    def from_right(t):
+        return copy(1, t, z + 1 + t // C, z - 1)
+
+    def goes_right(t):
+        return (t >= 0) & (t < T) & (z < n - 1) & (t // C <= z)
+
+    def goes_left(t):
+        return (t >= 0) & (t < T) & (z > 0) & (z + t // C <= n - 1)
+
+    def comes_left(t):
+        return (t >= 0) & (t < T) & (z - 1 - t // C >= 0)
+
+    def comes_right(t):
+        return (t >= 0) & (t < T) & (z + 1 + t // C <= n - 1)
+
+    def reduce_copy(block, g):
+        return pltpu.make_async_remote_copy(
+            src_ref=stage.at[block, pl.ds(pl.multiple_of(g * GR, GR), GR), :],
+            dst_ref=red.at[l, pl.ds(pl.multiple_of(g * GR, GR), GR), :],
+            send_sem=rsend_sem.at[block, g], recv_sem=rrecv_sem.at[l, g],
+            device_id={"lay": block}, device_id_type=MESH)
+
+    def scores(block, g, count):
+        first = pl.multiple_of(block * rows + g * GR, GR)
+        part = q_all[pl.ds(first, count * GR), :]
+        total = dot(part, tp_hi[...]) + dot(part, tp_lo[...])
+
+        @pl.when(block == l)
+        def _():
+            red[l, pl.ds(pl.multiple_of(g * GR, GR), count * GR), :] = total
+
+        @pl.when(block != l)
+        def _():
+            stage[block, pl.ds(pl.multiple_of(g * GR, GR), count * GR), :] = total
+            for k in range(count):
+                reduce_copy(block, g + k).start()
+
+    def turn_in(i, carry):
+        at = pl.multiple_of(i * TILE, TILE)
+        x = dot(t_ref[:, pl.ds(at, TILE)], perm[...], ((0,), (0,))).astype(bf16)
+        x = dot(diag[0], x) + dot(diag[1], x)
+        for h in range(cols // 128):
+            x_ref[h, pl.ds(at, TILE), :] = x[:, h * 128:(h + 1) * 128]
+        return carry
+
+    group = TILE // SIDE
+
+    def turn_out(i, carry):
+        halves = []
+        for h in range(cols // 128):
+            halves.append(jnp.concatenate(
+                [x_ref[h, pl.ds(i * group + k, SIDE, stride=SIDE), :] for k in range(group)], axis=0))
+        x = jnp.concatenate(halves, axis=1)
+        x = dot3(diag[2], diag[3], x)
+        lane = lax.broadcasted_iota(jnp.int32, (TILE, SIDE), 1)
+        which = lax.broadcasted_iota(jnp.int32, (TILE, SIDE), 0) // SIDE + i * group
+        values = jnp.concatenate([sp_ref[...]] * group, axis=0)
+        column = jnp.sum(jnp.where(lane == which, values, 0.0), axis=1, keepdims=True)
+        x = x * (1.0 / (column + damping))
+        x = dot3(diag[4], diag[5], x)
+        for h in range(cols // 128):
+            for k in range(group):
+                x_ref[h, pl.ds(i * group + k, SIDE, stride=SIDE), :] = (
+                    x[k * SIDE:(k + 1) * SIDE, h * 128:(h + 1) * 128])
+        return carry
+
+    def turn_back(i, carry):
+        at = pl.multiple_of(i * TILE, TILE)
+        x = jnp.concatenate(
+            [x_ref[h, pl.ds(at, TILE), :] for h in range(cols // 128)], axis=1)
+        hi, lo = split(dot3(diag[6], diag[7], x))
+        tp_hi[pl.ds(at, TILE), :] = hi
+        tp_lo[pl.ds(at, TILE), :] = lo
+        return carry
+
+    def step(t, carry):
+        for goes, send in ((goes_right, send_right), (goes_left, send_left)):
+            @pl.when(goes(t - 2))
+            def _():
+                send(t - 2).wait_send()
+
+            @pl.when(goes(t))
+            def _():
+                send(t).start()
+
+        @pl.when(t < 2)
+        def _():
+            lax.fori_loop(t * (tiles // 2), (t + 1) * (tiles // 2), turn_in, 0)
+
+        @pl.when((t >= 2) & (t < 6))
+        def _():
+            lax.fori_loop((t - 2) * (tiles // 4), (t - 1) * (tiles // 4), turn_out, 0)
+
+        @pl.when((t >= 6) & (t < 8))
+        def _():
+            lax.fori_loop((t - 6) * (tiles // 2), (t - 5) * (tiles // 2), turn_back, 0)
+
+        r = t - 1
+        for comes, got in ((comes_left, from_left), (comes_right, from_right)):
+            @pl.when(comes(r))
+            def _():
+                got(r).wait_recv()
+
+        early = jnp.where(t == C, z, jnp.where(t == C + 1, z - 1, z + 1))
+
+        @pl.when((t >= C) & (t <= C + 2) & (early >= 0) & (early < n))
+        def _():
+            scores(early, 0, G)
+
+        last = lax.rem(r, GR // CH) == GR // CH - 1
+        for comes, sign in ((comes_left, -1), (comes_right, 1)):
+            @pl.when((r >= C) & last & comes(r))
+            def _():
+                scores(z + sign * (1 + r // C), lax.rem(r, C) // (GR // CH), 1)
+        return carry
+
+    lax.fori_loop(0, T + 2, step, 0)
+
+    for k in range(1, n):
+        other = lax.rem(l + k, n)
+        for g in range(G):
+            reduce_copy(other, g).wait_send()
+            pltpu.make_async_remote_copy(
+                src_ref=stage.at[other, pl.ds(g * GR, GR), :],
+                dst_ref=red.at[other, pl.ds(g * GR, GR), :],
+                send_sem=rsend_sem.at[other, g], recv_sem=rrecv_sem.at[other, g],
+                device_id={"lay": other}, device_id_type=MESH).wait_recv()
+    total = red[0]
+    for k in range(1, n):
+        total = total + red[k]
+    o_ref[...] = total * score_scale
+
+
+def per_device(n, query_grads, train_grads, basis_out, basis_in, spectrum, train_ids):
+    rows, lay_count, width = query_grads.shape
+    cols = train_grads.shape[0]
+    C = rows // CH
+    T = (n - 1) * C
+    vmem = pl.BlockSpec(memory_space=pltpu.VMEM)
+    hbm = pl.BlockSpec(memory_space=pl.ANY)
+    return pl.pallas_call(
+        functools.partial(kernel, n),
+        out_shape=jax.ShapeDtypeStruct((rows, cols), f32),
+        in_specs=[hbm, hbm, vmem, vmem, vmem, vmem],
+        out_specs=vmem,
+        scratch_shapes=[
+            pltpu.VMEM((n * rows, width), bf16),
+            pltpu.VMEM((cols, width), bf16),
+            pltpu.VMEM((cols // 128, width, 128), f32),
+            pltpu.VMEM((width, cols), bf16),
+            pltpu.VMEM((width, cols), bf16),
+            pltpu.VMEM((cols, cols), bf16),
+            pltpu.VMEM((8, TILE, TILE), bf16),
+            pltpu.VMEM((n, rows, cols), f32),
+            pltpu.VMEM((n, rows, cols), f32),
+            pltpu.SemaphoreType.DMA((2,)),
+            pltpu.SemaphoreType.DMA((2, T)),
+            pltpu.SemaphoreType.DMA((2, T)),
+            pltpu.SemaphoreType.DMA((n, rows // GR)),
+            pltpu.SemaphoreType.DMA((n, rows // GR)),
+        ],
+        compiler_params=pltpu.CompilerParams(
+            collective_id=0, has_side_effects=True, vmem_limit_bytes=48 * 1024 * 1024),
+    )(
+        query_grads.reshape(rows, width),
+        train_grads.reshape(cols, width),
+        basis_out.reshape(SIDE, SIDE),
+        basis_in.reshape(SIDE, SIDE),
+        spectrum.reshape(SIDE, SIDE),
+        train_ids,
+    )
+
+
 def solution(mesh):
     in_specs = (
         P(("parts", "blk"), "lay", None),
@@ -48,6 +322,6 @@
         P(("parts", "blk"), None),
     )
     out_specs = P(("parts", "lay"), "blk")
-    return jax.shard_map(
-        per_device, mesh=mesh, in_specs=in_specs, out_specs=out_specs, check_vma=False
-    )
+    n = mesh.shape["blk"]
+    body = functools.partial(per_device, n) if n == mesh.shape["lay"] else plain
+    return jax.shard_map(body, mesh=mesh, in_specs=in_specs, out_specs=out_specs, check_vma=False)

time: 139 us -> 94 us (0.68)
  waiting for transfers between devices: 103 us -> 0 us
  Pallas kernels: 0 us -> 85.9 us
  matrix products: 17.4 us -> 0 us
  between operations: 13.5 us -> 0.02 us
  local copies, waits for them, and re-layouts: 3.44 us -> 6.25 us
    pallas_call x0 -> x1, Pallas kernels: none -> 85.9 us  [per_device(): pl.pallas_call(functools.partial(kernel, n), out_shape=jax.ShapeDtypeStru...]
    all_gather x1 -> x0, waiting for transfers between devices: 83.4 us -> none  [per_device(): all_queries = lax.all_gather(prepared, 'blk', axis=0, tiled=True)]
    reduce_scatter x1 -> x0, waiting for transfers between devices: 20 us -> none  [per_device(): lax.psum_scatter(lax.dot_general(all_queries, local_rows, (((1,), (1,)),...]
    dot_general x5 -> x0, matrix products: 17.4 us -> none  [the longest x1 4.3 us: per_device(): lax.dot_general(all_queries, local_rows, (((1,), (1,)), ((), ())), prefer...]
    unnamed x11 -> x12, local copies, waits for them, and re-layouts: 1.79 us -> 6.18 us
    unnamed x0 -> x1, other arithmetic: none -> 1.4 us
  transfers between devices with their start and end apart: 2 -> 0, of which waited for: 2 -> 0; matrix products, arithmetic and copies ran while one was open for 0% -> 0% of each run, Pallas kernels for 0% -> 0%
where the time goes in v1:
time: 94 us; the launch traced here: 93.6 us
  Pallas kernels  85.9 us (91%)
  local copies, waits for them, and re-layouts  6.25 us (7%)
  other arithmetic  1.4 us (1%)
    pallas_call x1, Pallas kernels, per_device(): pl.pallas_call(functools.partial(kernel, n), out_shape=jax.ShapeDtypeStru...  85.9 us
    unnamed x12, local copies, waits for them, and re-layouts  6.18 us

profile of v1, /device:TPU:0, one launch (start us, length us, event | category | flops | bytes accessed | tf_op | source)
XLA Modules:
  0.0 93.6 jit_solution(15368822628550368857)
XLA Ops:
  0.0 0.5 broadcast.3
  0.5 1.4 %reduce.3 = f32[4096]{0:T(1024)S(1)} reduce(f32[1,4096]{1,0:T(1,128)} %param.10, f32[]{:T(128)} %broadcast.3), dimensions={0}, to_apply=%param.10.reduce_sub_computation.3 | reduce | bytes 32772 | tf_op args[4]
  1.9 0.1 reshape.19.sp_ref
  2.0 0.0 copy-start
  2.0 1.6 %copy-done = bf16[256,1,4096]{2,0,1:T(8,128)(2,1)S(1)} copy-done((bf16[256,1,4096]{2,0,1:T(8,128)(2,1)S(1)}, bf16[256,1,4096]{2,0,1:T(8,128)(2,1)}, u32[]{:S(2)}) %copy-start) | copy-done | bytes 2097176
  3.6 0.0 copy-start.1
  3.6 1.2 %copy-done.1 = bf16[128,1,4096]{2,0,1:T(8,128)(2,1)S(1)} copy-done((bf16[128,1,4096]{2,0,1:T(8,128)(2,1)S(1)}, bf16[128,1,4096]{2,0,1:T(8,128)(2,1)}, u32[]{:S(2)}) %copy-start.1) | copy-done | bytes 1048600
  4.8 0.0 copy-start.2
  4.8 0.8 copy-done.2
  5.6 0.0 copy-start.3
  5.6 0.8 copy-done.3
  6.3 0.0 copy-start.4
  6.3 0.7 copy-done.4
  7.0 85.9 %shard_map.64 = f32[128,256]{1,0:T(8,128)S(1)} custom-call(bf16[128,4096]{1,0:T(8,128)(2,1)S(1)} %bitcast.5, bf16[256,4096]{1,0:T(8,128)(2,1)S(1)} %bitcast.4, f32[64,64]{1,0:T(8,128)S(1)} %bitcast.6, f32[64,64]{1,0:T(8,128)S(1)} %bitcast.7, f32[64,64]{1,0:T(8,128)S(1)} %reshape.19.sp_ref, s32[1,256]{1,0:T(1,128)S(1)} %copy-done.4), custom_call_target="tpu_custom_call" | custom-call | tf_op jit(solution)/shard_map/pallas_call | solution.py:282
  92.9 0.7 copy.8
Async XLA Ops:
  2.0 1.6 %copy-start = (bf16[256,1,4096]{2,0,1:T(8,128)(2,1)S(1)}, bf16[256,1,4096]{2,0,1:T(8,128)(2,1)}, u32[]{:S(2)}) copy-start(bf16[256,1,4096]{2,0,1:T(8,128)(2,1)} %param.7) | copy-start | bytes 6291460
  3.6 1.2 %copy-start.1 = (bf16[128,1,4096]{2,0,1:T(8,128)(2,1)S(1)}, bf16[128,1,4096]{2,0,1:T(8,128)(2,1)}, u32[]{:S(2)}) copy-start(bf16[128,1,4096]{2,0,1:T(8,128)(2,1)} %param.6) | copy-start | bytes 3145732
  4.8 0.8 copy-start.2
  5.6 0.8 copy-start.3
  6.3 0.7 copy-start.4

commit v2 on v1

v2 whole, which is shorter than its diff:
```python
import functools

import jax
import jax.numpy as jnp
from jax import lax
from jax.experimental import pallas as pl
from jax.experimental.pallas import tpu as pltpu
from jax.sharding import PartitionSpec as P

damping = 0.1
score_scale = 1.0 / 256.0
MESH = pl.DeviceIdType.MESH
f32 = jnp.float32
bf16 = jnp.bfloat16


def precondition(grads, basis_out, basis_in, spectrum):
    row_count = grads.shape[0]
    lay_count = grads.shape[1]
    out_dim = basis_out.shape[1]
    in_dim = basis_in.shape[1]
    field = grads.astype(jnp.float32).reshape(row_count, lay_count, out_dim, in_dim)
    high = lax.Precision.HIGHEST
    rotated = jnp.einsum("lap,mlab->mlpb", basis_out, field, precision=high)
    rotated = jnp.einsum("mlpb,lbr->mlpr", rotated, basis_in, precision=high)
    scaled = rotated / (spectrum.reshape(1, lay_count, out_dim, in_dim) + damping)
    restored = jnp.einsum("lap,mlpr->mlar", basis_out, scaled, precision=high)
    restored = jnp.einsum("mlar,lbr->mlab", restored, basis_in, precision=high)
    return restored.reshape(row_count, lay_count * out_dim * in_dim).astype(jnp.bfloat16)


def plain(query_grads, train_grads, basis_out, basis_in, spectrum, train_ids):
    prepared = precondition(query_grads, basis_out, basis_in, spectrum)
    local_rows = train_grads.reshape(train_grads.shape[0], -1)
    all_queries = lax.all_gather(prepared, "blk", axis=0, tiled=True)
    summed = lax.psum_scatter(
        lax.dot_general(
            all_queries, local_rows, (((1,), (1,)), ((), ())), preferred_element_type=jnp.float32
        ),
        "lay",
        scatter_dimension=0,
        tiled=True,
    )
    scaled_scores = summed * score_scale
    return jnp.take(scaled_scores, train_ids[0], axis=1)


def dot(a, b, dims=((1,), (0,))):
    return lax.dot_general(a, b, (dims, ((), ())), preferred_element_type=f32)


def split(x):
    hi = x.astype(bf16)
    return hi, (x - hi.astype(f32)).astype(bf16)


def dot3(a_hi, a_lo, b):
    b_hi, b_lo = split(b)
    return dot(a_hi, b_hi) + (dot(a_hi, b_lo) + dot(a_lo, b_hi))


CH = 16
GR = 64
SIDE = 64
TILE = 256
MOVED = 7


def kernel(n, q_hbm, t_hbm, bo_hbm, bi_hbm, sp_hbm, ids_hbm, o_ref,
           q_all, t_ref, bo_ref, bi_ref, sp_ref, ids_ref, sq_ref,
           x_ref, tp_hi, tp_lo, tp_end, perm, diag, stage, red, estage, ered,
           load_sem, a_send, a_recv, b_send, b_recv, c_send, c_recv,
           e_send, e_recv, r_send, r_recv):
    z = lax.axis_index("blk")
    l = lax.axis_index("lay")
    rows = q_hbm.shape[0]
    cols = t_ref.shape[0]
    width = q_hbm.shape[1]
    tiles = width // TILE
    C = rows // CH
    G = rows // GR
    KF = MOVED * TILE
    low = z < n // 2
    end = jnp.where(low, 0, n - 1)
    mid = jnp.where(low, 1, n - 2)
    far_mid = n - 1 - mid
    far_end = n - 1 - end
    at_end = z == end
    at_mid = z == mid

    def place(block, row, count, unit):
        return pl.ds(pl.multiple_of(block * rows + row, unit), count)

    loads = [
        pltpu.make_async_copy(q_hbm, q_all.at[place(z, 0, rows, rows), :], load_sem.at[0]),
        pltpu.make_async_copy(bo_hbm, bo_ref, load_sem.at[1]),
        pltpu.make_async_copy(bi_hbm, bi_ref, load_sem.at[2]),
        pltpu.make_async_copy(sp_hbm, sp_ref, load_sem.at[3]),
        pltpu.make_async_copy(ids_hbm, ids_ref, load_sem.at[4]),
        pltpu.make_async_copy(t_hbm, t_ref, load_sem.at[5]),
    ]
    for load in loads:
        load.start()

    barrier = pltpu.get_barrier_semaphore()
    partner = jnp.where(at_end, mid, end)
    for k in range(n):
        pl.semaphore_signal(
            barrier, inc=1, device_id={"blk": partner, "lay": k}, device_id_type=MESH)
    for k in range(1, n):
        pl.semaphore_signal(
            barrier, inc=1, device_id={"lay": lax.rem(l + k, n)}, device_id_type=MESH)

    @pl.when(at_mid)
    def _():
        pl.semaphore_signal(barrier, inc=1, device_id={"blk": far_mid}, device_id_type=MESH)

    def remote(src, dst, send, recv, target):
        return pltpu.make_async_remote_copy(
            src_ref=src, dst_ref=dst, send_sem=send, recv_sem=recv,
            device_id=target, device_id_type=MESH)

    def a_query(t):
        part = q_all.at[place(end, t * CH, CH, CH), :]
        return remote(part, part, a_send.at[t], a_recv.at[t], {"blk": mid})

    def a_train(m):
        piece = pl.ds(pl.multiple_of(m * TILE, TILE), TILE)
        return remote(tp_hi.at[piece, :], tp_end.at[piece, :],
                      a_send.at[C + m], a_recv.at[C + m], {"blk": mid})

    def b_out(t):
        part = q_all.at[place(jnp.where(t < C, mid, end), lax.rem(t, C) * CH, CH, CH), :]
        return remote(part, part, b_send.at[t], b_recv.at[t], {"blk": far_mid})

    def b_in(t):
        part = q_all.at[place(jnp.where(t < C, far_mid, far_end), lax.rem(t, C) * CH, CH, CH), :]
        return remote(part, part, b_send.at[t], b_recv.at[t], {"blk": far_mid})

    def c_own(t):
        part = q_all.at[place(mid, t * CH, CH, CH), pl.ds(KF, width - KF)]
        return remote(part, part, c_send.at[t], c_recv.at[t], {"blk": end})

    def c_far(t):
        part = q_all.at[place(jnp.where(t < C, far_mid, far_end), lax.rem(t, C) * CH, CH, CH),
                        pl.ds(KF, width - KF)]
        return remote(part, part, c_send.at[C + t], c_recv.at[C + t], {"blk": end})

    def e_copy(block, g, sender):
        part = pl.ds(pl.multiple_of(g * GR, GR), GR)
        return remote(estage.at[block, part, :], ered.at[sender, part, :],
                      e_send.at[block, g], e_recv.at[sender, g], {"blk": end, "lay": block})

    def r_copy(block, g, sender):
        part = pl.ds(pl.multiple_of(g * GR, GR), GR)
        return remote(stage.at[block, part, :], red.at[sender, part, :],
                      r_send.at[block, g], r_recv.at[sender, g], {"lay": block})

    for load in loads[1:5]:
        load.wait()
    row_i = lax.broadcasted_iota(jnp.int32, (TILE, SIDE), 0)
    col_i = lax.broadcasted_iota(jnp.int32, (TILE, SIDE), 1)
    pick = jnp.where(lax.rem(row_i, SIDE) == col_i, 1.0, 0.0).astype(bf16)
    big_r = lax.broadcasted_iota(jnp.int32, (TILE, TILE), 0)
    big_c = lax.broadcasted_iota(jnp.int32, (TILE, TILE), 1)
    same = big_r // SIDE == big_c // SIDE
    group = TILE // SIDE

    def spread(base, side):
        half = dot(pick, base, ((1,), (side,))).astype(bf16)
        full = dot(half, pick, ((1,), (1,)))
        return jnp.where(same, full, 0.0).astype(bf16)

    def prepare():
        for k, (ref, side) in enumerate(((bi_ref, 1), (bo_ref, 1), (bo_ref, 0), (bi_ref, 0))):
            hi, lo = split(ref[0])
            diag[2 * k] = spread(hi, side)
            diag[2 * k + 1] = spread(lo, side)
        perm[...] = jnp.where(big_r == ids_ref[...], 1.0, 0.0).astype(bf16)
        for p in range(SIDE):
            sq_ref[p:p + 1, :] = 1.0 / (sp_ref[:, p * SIDE:(p + 1) * SIDE] + damping)

    loads[0].wait()
    loads[5].wait()
    pl.semaphore_wait(barrier, 2 * n - 1 + at_mid.astype(jnp.int32))

    def scores(block, g, count, first=0):
        here = place(block, g * GR, count * GR, GR)
        part = q_all[here, first:]
        total = dot(part, tp_hi[first:, :]) + dot(part, tp_lo[first:, :])
        span = pl.ds(pl.multiple_of(g * GR, GR), count * GR)

        @pl.when(block == l)
        def _():
            red[l, span, :] = total

        @pl.when(block != l)
        def _():
            stage[block, span, :] = total
            for k in range(count):
                r_copy(block, g + k, l).start()

    def moved_scores(block, g, count):
        part = q_all[place(block, g * GR, count * GR, GR), :KF]
        span = pl.ds(pl.multiple_of(g * GR, GR), count * GR)
        estage[block, span, :] = dot(part, tp_end[...]).astype(bf16)
        for k in range(count):
            e_copy(block, g + k, l).start()

    def turn_in(i, carry):
        at = pl.multiple_of(i * TILE, TILE)
        x = dot(t_ref[:, pl.ds(at, TILE)], perm[...], ((0,), (0,))).astype(bf16)
        x = dot(diag[0], x) + dot(diag[1], x)
        for h in range(cols // 128):
            x_ref[h, pl.ds(at, TILE), :] = x[:, h * 128:(h + 1) * 128]
        return carry

    def turn_out(i, carry):
        halves = []
        for h in range(cols // 128):
            halves.append(jnp.concatenate(
                [x_ref[h, pl.ds(i * group + k, SIDE, stride=SIDE), :] for k in range(group)], axis=0))
        x = jnp.concatenate(halves, axis=1)
        x = dot3(diag[2], diag[3], x)
        lane = lax.broadcasted_iota(jnp.int32, (TILE, SIDE), 1)
        which = lax.broadcasted_iota(jnp.int32, (TILE, SIDE), 0) // SIDE + i * group
        values = jnp.concatenate([sq_ref[...]] * group, axis=0)
        x = x * jnp.sum(jnp.where(lane == which, values, 0.0), axis=1, keepdims=True)
        x = dot3(diag[4], diag[5], x)
        for h in range(cols // 128):
            for k in range(group):
                x_ref[h, pl.ds(i * group + k, SIDE, stride=SIDE), :] = (
                    x[k * SIDE:(k + 1) * SIDE, h * 128:(h + 1) * 128])
        return carry

    def turn_back(i, carry):
        at = pl.multiple_of(i * TILE, TILE)
        x = jnp.concatenate(
            [x_ref[h, pl.ds(at, TILE), :] for h in range(cols // 128)], axis=1)
        hi, lo = split(dot3(diag[6], diag[7], x))
        tp_hi[pl.ds(at, TILE), :] = hi
        tp_lo[pl.ds(at, TILE), :] = lo
        return carry

    LAG = 3
    PER = GR // CH

    def when(*parts):
        test = parts[0]
        for part in parts[1:]:
            test = test & part
        return pl.when(test)

    def within(t, first, last):
        return (t >= first) & (t < last)

    def step(t, carry):
        @when(at_end, within(t - LAG, 0, C))
        def _():
            a_query(t - LAG).wait_send()

        @when(at_end, within(t - LAG, C, C + MOVED))
        def _():
            a_train(t - LAG - C).wait_send()

        @when(at_end, t < C)
        def _():
            a_query(t).start()

        @when(at_end, within(t, C, C + MOVED))
        def _():
            a_train(t - C).start()

        @when(at_mid, within(t - LAG, 0, 2 * C))
        def _():
            b_out(t - LAG).wait_send()

        @when(at_mid, t < 2 * C)
        def _():
            b_out(t).start()

        even = lax.rem(t, 2) == 0

        @when(at_mid, even, t < 2 * C)
        def _():
            c_own(t // 2).start()

        @pl.when(t == 0)
        def _():
            prepare()

        @pl.when(t < 2)
        def _():
            lax.fori_loop(t * (tiles // 2), (t + 1) * (tiles // 2), turn_in, 0)

        @pl.when(within(t, 2, 6))
        def _():
            lax.fori_loop((t - 2) * (tiles // 4), (t - 1) * (tiles // 4), turn_out, 0)

        @pl.when(within(t, 6, 8))
        def _():
            lax.fori_loop((t - 6) * (tiles // 2), (t - 5) * (tiles // 2), turn_back, 0)

        @when(at_mid, within(t - 1, 0, C))
        def _():
            a_query(t - 1).wait_recv()

        @when(at_mid, within(t - 1, C, C + MOVED))
        def _():
            a_train(t - 1 - C).wait_recv()

        @when(at_mid, within(t - 1, 0, 2 * C))
        def _():
            b_in(t - 1).wait_recv()
            c_far(t - 1).start()

        @when(at_end, within(t - 1, 0, 2 * C), ~even)
        def _():
            c_own((t - 1) // 2).wait_recv()

        @when(at_end, within(t - 2, 0, 2 * C))
        def _():
            c_far(t - 2).wait_recv()

        early = jnp.where(t == C, mid, jnp.where(t == C + 1, end, far_mid))

        @when(at_mid, within(t, C, C + 3))
        def _():
            scores(early, 0, G)

        @when(at_mid, within(t - 1, C, 2 * C), lax.rem(t - 1, PER) == PER - 1)
        def _():
            scores(far_end, lax.rem(t - 1, C) // PER, 1)

        @when(at_mid, t == C + MOVED)
        def _():
            moved_scores(mid, 0, G)
            moved_scores(far_mid, 0, G)
            moved_scores(far_end, 0, 1)

        @when(at_mid, t == 2 * C)
        def _():
            moved_scores(far_end, 1, 1)

        @when(at_end, t == C)
        def _():
            scores(end, 0, G)

        @when(at_end, t == C + 2)
        def _():
            scores(far_mid, 0, G, KF)

        @when(at_end, t == 2 * C)
        def _():
            scores(mid, 0, G, KF)

        @when(at_end, within(t - 2, C, 2 * C), lax.rem(t - 2, PER) == PER - 1)
        def _():
            scores(far_end, lax.rem(t - 2, C) // PER, 1, KF)
        return carry

    lax.fori_loop(0, 2 * C + LAG, step, 0)

    @pl.when(at_mid)
    def _():
        def sent(t, carry):
            c_far(t).wait_send()
            return carry

        def sent_own(t, carry):
            c_own(t).wait_send()
            return carry

        lax.fori_loop(0, 2 * C, sent, 0)
        lax.fori_loop(0, C, sent_own, 0)
        for block in (mid, far_mid, far_end):
            for g in range(G):
                e_copy(block, g, l).wait_send()

    for k in range(1, n):
        other = lax.rem(l + k, n)
        for g in range(G):
            r_copy(other, g, l).wait_send()
            r_copy(other, g, other).wait_recv()
    total = red[0]
    for k in range(1, n):
        total = total + red[k]
    o_ref[...] = total * score_scale

    @pl.when(at_end & (l != end))
    def _():
        for k in range(n):
            for g in range(G):
                e_copy(l, g, k).wait_recv()
        extra = ered[0].astype(f32)
        for k in range(1, n):
            extra = extra + ered[k].astype(f32)
        o_ref[...] += extra * score_scale


def per_device(n, query_grads, train_grads, basis_out, basis_in, spectrum, train_ids):
    rows, lay_count, width = query_grads.shape
    cols = train_grads.shape[0]
    C = rows // CH
    G = rows // GR
    hbm = pl.BlockSpec(memory_space=pl.ANY)
    dma = pltpu.SemaphoreType.DMA
    return pl.pallas_call(
        functools.partial(kernel, n),
        out_shape=jax.ShapeDtypeStruct((rows, cols), f32),
        in_specs=[hbm] * 6,
        out_specs=pl.BlockSpec(memory_space=pltpu.VMEM),
        scratch_shapes=[
            pltpu.VMEM((n * rows, width), bf16),
            pltpu.VMEM((cols, width), bf16),
            pltpu.VMEM((1, SIDE, SIDE), f32),
            pltpu.VMEM((1, SIDE, SIDE), f32),
            pltpu.VMEM((1, width), f32),
            pltpu.VMEM((1, cols), jnp.int32),
            pltpu.VMEM((SIDE, SIDE), f32),
            pltpu.VMEM((cols // 128, width, 128), f32),
            pltpu.VMEM((width, cols), bf16),
            pltpu.VMEM((width, cols), bf16),
            pltpu.VMEM((MOVED * TILE, cols), bf16),
            pltpu.VMEM((cols, cols), bf16),
            pltpu.VMEM((8, TILE, TILE), bf16),
            pltpu.VMEM((n, rows, cols), f32),
            pltpu.VMEM((n, rows, cols), f32),
            pltpu.VMEM((n, rows, cols), bf16),
            pltpu.VMEM((n, rows, cols), bf16),
            dma((6,)),
            dma((C + MOVED,)),
            dma((C + MOVED,)),
            dma((2 * C,)),
            dma((2 * C,)),
            dma((3 * C,)),
            dma((3 * C,)),
            dma((n, G)),
            dma((n, G)),
            dma((n, G)),
            dma((n, G)),
        ],
        compiler_params=pltpu.CompilerParams(
            collective_id=0, has_side_effects=True, vmem_limit_bytes=60 * 1024 * 1024),
    )(
        query_grads.reshape(rows, width),
        train_grads.reshape(cols, width),
        basis_out,
        basis_in,
        spectrum,
        train_ids,
    )


def solution(mesh):
    in_specs = (
        P(("parts", "blk"), "lay", None),
        P(("parts", "blk"), "lay", None),
        P("lay", None, None),
        P("lay", None, None),
        P("lay", None),
        P(("parts", "blk"), None),
    )
    out_specs = P(("parts", "lay"), "blk")
    n = mesh.shape["blk"]
    body = functools.partial(per_device, n) if n == mesh.shape["lay"] == 4 else plain
    return jax.shard_map(body, mesh=mesh, in_specs=in_specs, out_specs=out_specs, check_vma=False)
```

time: 94 us -> 73.8 us (0.79)
  Pallas kernels: 85.9 us -> 72 us
  local copies, waits for them, and re-layouts: 6.25 us -> 1.57 us
  other arithmetic: 1.4 us -> 0 us
    pallas_call x1, Pallas kernels: 85.9 us -> 72 us  [per_device(): pl.pallas_call(functools.partial(kernel, n), out_shape=jax.ShapeDtypeStru...]
    unnamed x12 -> x1, local copies, waits for them, and re-layouts: 6.18 us -> 1.57 us
    unnamed x1 -> x0, other arithmetic: 1.4 us -> none
where the time goes in v2:
time: 73.8 us; the launch traced here: 73.6 us
  Pallas kernels  72 us (98%)
  local copies, waits for them, and re-layouts  1.57 us (2%)
    pallas_call x1, Pallas kernels, per_device(): pl.pallas_call(functools.partial(kernel, n), out_shape=jax.ShapeDtypeStru...  72 us
    unnamed x1, local copies, waits for them, and re-layouts  1.57 us

profile of v2, /device:TPU:0, one launch (start us, length us, event | category | flops | bytes accessed | tf_op | source)
XLA Modules:
  0.0 73.6 jit_solution(15061042982764957060)
XLA Ops:
  0.0 72.0 %shard_map.64 = f32[128,256]{1,0:T(8,128)} custom-call(bf16[128,4096]{1,0:T(8,128)(2,1)} %bitcast.3, bf16[256,4096]{1,0:T(8,128)(2,1)} %bitcast.2, f32[1,64,64]{2,1,0:T(8,128)} %bo_hbm.1, f32[1,64,64]{2,1,0:T(8,128)} %bi_hbm.1, f32[1,4096]{1,0:T(1,128)} %sp_hbm.1, s32[1,256]{1,0:T(1,128)} %ids_hbm.1), custom_call_target="tpu_custom_call" | custom-call | tf_op jit(solution)/shard_map/pallas_call | solution.py:408
  72.1 1.6 %copy.8 = f32[128,256]{1,0:T(8,128)} copy(f32[128,256]{1,0:T(8,128)} %shard_map.64) | data formatting | bytes 262144

commit v3 on v2

--- a/solution.py
+++ b/solution.py
@@ -181,7 +181,6 @@
             sq_ref[p:p + 1, :] = 1.0 / (sp_ref[:, p * SIDE:(p + 1) * SIDE] + damping)
 
     loads[0].wait()
-    loads[5].wait()
     pl.semaphore_wait(barrier, 2 * n - 1 + at_mid.astype(jnp.int32))
 
     def scores(block, g, count, first=0):
@@ -243,6 +242,11 @@
         return carry
 
     LAG = 3
+    D = 2
+
+    def run(task, first, count):
+        lax.fori_loop(0, count, lambda j, carry: task(first + j, carry), 0, unroll=4)
+
     PER = GR // CH
 
     def when(*parts):
@@ -288,78 +292,83 @@
         @pl.when(t == 0)
         def _():
             prepare()
+            loads[5].wait()
 
         @pl.when(t < 2)
         def _():
-            lax.fori_loop(t * (tiles // 2), (t + 1) * (tiles // 2), turn_in, 0)
+            run(turn_in, t * (tiles // 2), tiles // 2)
 
         @pl.when(within(t, 2, 6))
         def _():
-            lax.fori_loop((t - 2) * (tiles // 4), (t - 1) * (tiles // 4), turn_out, 0)
+            run(turn_out, (t - 2) * (tiles // 4), tiles // 4)
 
         @pl.when(within(t, 6, 8))
         def _():
-            lax.fori_loop((t - 6) * (tiles // 2), (t - 5) * (tiles // 2), turn_back, 0)
-
-        @when(at_mid, within(t - 1, 0, C))
-        def _():
-            a_query(t - 1).wait_recv()
-
-        @when(at_mid, within(t - 1, C, C + MOVED))
-        def _():
-            a_train(t - 1 - C).wait_recv()
-
-        @when(at_mid, within(t - 1, 0, 2 * C))
-        def _():
-            b_in(t - 1).wait_recv()
-            c_far(t - 1).start()
-
-        @when(at_end, within(t - 1, 0, 2 * C), ~even)
-        def _():
-            c_own((t - 1) // 2).wait_recv()
-
-        @when(at_end, within(t - 2, 0, 2 * C))
-        def _():
-            c_far(t - 2).wait_recv()
-
-        early = jnp.where(t == C, mid, jnp.where(t == C + 1, end, far_mid))
-
-        @when(at_mid, within(t, C, C + 3))
+            run(turn_back, (t - 6) * (tiles // 2), tiles // 2)
+
+        r = t - D
+
+        @when(at_mid, within(r, 0, C))
+        def _():
+            a_query(r).wait_recv()
+
+        @when(at_mid, within(r, C, C + MOVED))
+        def _():
+            a_train(r - C).wait_recv()
+
+        @when(at_mid, within(r, 0, 2 * C))
+        def _():
+            b_in(r).wait_recv()
+            c_far(r).start()
+
+        e = r - 1
+
+        @when(at_end, within(e, 0, 2 * C), lax.rem(e, 2) == 0)
+        def _():
+            c_own(e // 2).wait_recv()
+
+        @when(at_end, within(e, 0, 2 * C))
+        def _():
+            c_far(e).wait_recv()
+
+        early = jnp.where(r == C - 1, mid, jnp.where(r == C, end, far_mid))
+
+        @when(at_mid, within(r, C - 1, C + 2))
         def _():
             scores(early, 0, G)
 
-        @when(at_mid, within(t - 1, C, 2 * C), lax.rem(t - 1, PER) == PER - 1)
-        def _():
-            scores(far_end, lax.rem(t - 1, C) // PER, 1)
-
-        @when(at_mid, t == C + MOVED)
+        @when(at_mid, r == C + MOVED - 1)
         def _():
             moved_scores(mid, 0, G)
             moved_scores(far_mid, 0, G)
             moved_scores(far_end, 0, 1)
 
-        @when(at_mid, t == 2 * C)
+        @when(at_mid, r == 2 * C - 1)
         def _():
             moved_scores(far_end, 1, 1)
 
-        @when(at_end, t == C)
+        @when(at_mid, within(r, C, 2 * C), lax.rem(r, PER) == PER - 1)
+        def _():
+            scores(far_end, lax.rem(r, C) // PER, 1)
+
+        @when(at_end, e == C - 2)
         def _():
             scores(end, 0, G)
 
-        @when(at_end, t == C + 2)
+        @when(at_end, e == C)
         def _():
             scores(far_mid, 0, G, KF)
 
-        @when(at_end, t == 2 * C)
+        @when(at_end, within(e, C, 2 * C), lax.rem(e, PER) == PER - 1)
+        def _():
+            scores(far_end, lax.rem(e, C) // PER, 1, KF)
+
+        @when(at_end, e == 2 * C - 2)
         def _():
             scores(mid, 0, G, KF)
-
-        @when(at_end, within(t - 2, C, 2 * C), lax.rem(t - 2, PER) == PER - 1)
-        def _():
-            scores(far_end, lax.rem(t - 2, C) // PER, 1, KF)
         return carry
 
-    lax.fori_loop(0, 2 * C + LAG, step, 0)
+    lax.fori_loop(0, 2 * C + LAG + 1, step, 0)
 
     @pl.when(at_mid)
     def _():

time: 73.8 us -> 64.1 us (0.87)
  Pallas kernels: 72 us -> 62.3 us
    pallas_call x1, Pallas kernels: 72 us -> 62.3 us  [per_device(): pl.pallas_call(functools.partial(kernel, n), out_shape=jax.ShapeDtypeStru...]
where the time goes in v3:
time: 64.1 us; the launch traced here: 63.9 us
  Pallas kernels  62.3 us (97%)
  local copies, waits for them, and re-layouts  1.57 us (2%)
    pallas_call x1, Pallas kernels, per_device(): pl.pallas_call(functools.partial(kernel, n), out_shape=jax.ShapeDtypeStru...  62.3 us
    unnamed x1, local copies, waits for them, and re-layouts  1.57 us

profile of v3, /device:TPU:0, one launch (start us, length us, event | category | flops | bytes accessed | tf_op | source)
XLA Modules:
  0.0 63.9 jit_solution(13791696330905260440)
XLA Ops:
  0.0 62.3 %shard_map.64 = f32[128,256]{1,0:T(8,128)} custom-call(bf16[128,4096]{1,0:T(8,128)(2,1)} %bitcast.3, bf16[256,4096]{1,0:T(8,128)(2,1)} %bitcast.2, f32[1,64,64]{2,1,0:T(8,128)} %bo_hbm.1, f32[1,64,64]{2,1,0:T(8,128)} %bi_hbm.1, f32[1,4096]{1,0:T(1,128)} %sp_hbm.1, s32[1,256]{1,0:T(1,128)} %ids_hbm.1), custom_call_target="tpu_custom_call" | custom-call | tf_op jit(solution)/shard_map/pallas_call | solution.py:417
  62.4 1.6 %copy.8 = f32[128,256]{1,0:T(8,128)} copy(f32[128,256]{1,0:T(8,128)} %shard_map.64) | data formatting | bytes 262144

commit v4 on v3

--- a/solution.py
+++ b/solution.py
@@ -68,7 +68,7 @@
 
 def kernel(n, q_hbm, t_hbm, bo_hbm, bi_hbm, sp_hbm, ids_hbm, o_ref,
            q_all, t_ref, bo_ref, bi_ref, sp_ref, ids_ref, sq_ref,
-           x_ref, tp_hi, tp_lo, tp_end, perm, diag, stage, red, estage, ered,
+           x_ref, tp_hi, tp_end, perm, diag, stage, red, estage, ered,
            load_sem, a_send, a_recv, b_send, b_recv, c_send, c_recv,
            e_send, e_recv, r_send, r_recv):
     z = lax.axis_index("blk")
@@ -186,7 +186,7 @@
     def scores(block, g, count, first=0):
         here = place(block, g * GR, count * GR, GR)
         part = q_all[here, first:]
-        total = dot(part, tp_hi[first:, :]) + dot(part, tp_lo[first:, :])
+        total = dot(part, tp_hi[first:, :])
         span = pl.ds(pl.multiple_of(g * GR, GR), count * GR)
 
         @pl.when(block == l)
@@ -236,9 +236,7 @@
         at = pl.multiple_of(i * TILE, TILE)
         x = jnp.concatenate(
             [x_ref[h, pl.ds(at, TILE), :] for h in range(cols // 128)], axis=1)
-        hi, lo = split(dot3(diag[6], diag[7], x))
-        tp_hi[pl.ds(at, TILE), :] = hi
-        tp_lo[pl.ds(at, TILE), :] = lo
+        tp_hi[pl.ds(at, TILE), :] = dot3(diag[6], diag[7], x).astype(bf16)
         return carry
 
     LAG = 3
@@ -428,7 +426,6 @@
             pltpu.VMEM((1, cols), jnp.int32),
             pltpu.VMEM((SIDE, SIDE), f32),
             pltpu.VMEM((cols // 128, width, 128), f32),
-            pltpu.VMEM((width, cols), bf16),
             pltpu.VMEM((width, cols), bf16),
             pltpu.VMEM((MOVED * TILE, cols), bf16),
             pltpu.VMEM((cols, cols), bf16),

time: 64.1 us -> 63.9 us (level)
  no operation moved by 1% of the time
where the time goes in v4:
time: 63.9 us; the launch traced here: 63.7 us
  Pallas kernels  62.1 us (97%)
  local copies, waits for them, and re-layouts  1.57 us (2%)
    pallas_call x1, Pallas kernels, per_device(): pl.pallas_call(functools.partial(kernel, n), out_shape=jax.ShapeDtypeStru...  62.1 us
    unnamed x1, local copies, waits for them, and re-layouts  1.57 us

profile of v4, /device:TPU:0, one launch (start us, length us, event | category | flops | bytes accessed | tf_op | source)
XLA Modules:
  0.0 63.7 jit_solution(10667851561913272086)
XLA Ops:
  0.0 62.1 %shard_map.64 = f32[128,256]{1,0:T(8,128)} custom-call(bf16[128,4096]{1,0:T(8,128)(2,1)} %bitcast.3, bf16[256,4096]{1,0:T(8,128)(2,1)} %bitcast.2, f32[1,64,64]{2,1,0:T(8,128)} %bo_hbm.1, f32[1,64,64]{2,1,0:T(8,128)} %bi_hbm.1, f32[1,4096]{1,0:T(1,128)} %sp_hbm.1, s32[1,256]{1,0:T(1,128)} %ids_hbm.1), custom_call_target="tpu_custom_call" | custom-call | tf_op jit(solution)/shard_map/pallas_call | solution.py:415
  62.2 1.6 %copy.8 = f32[128,256]{1,0:T(8,128)} copy(f32[128,256]{1,0:T(8,128)} %shard_map.64) | data formatting | bytes 262144
